TPU v7x, 32 devices: a whole 2x2x4 slice. The times are simulated.
32 devices in a mesh: layer: 4 (over z), col: 4 (over x, core), row: 2 (over y).
Axes of the slice: x: 2, y: 2, z: 4, core: 2. Of those that a mesh axis runs over, the one named last changes fastest.
Arguments:
- front_copies: bfloat16 [4, 3072, 3072], P('layer', 'row', 'col'), may hold values from -6 to 6
- lower_panels: bfloat16 [4, 2, 3072, 512], P('layer', None, 'row', 'col'), may hold values from -0.25 to 0.25
- upper_panels: bfloat16 [4, 2, 512, 3072], P('layer', None, 'row', 'col'), may hold values from -6 to 6
- diag_blocks: float32 [4, 2, 512, 512], P('layer'), may hold values from -2 to 4, as said below
- block_fill: int32 [4, 2, 24], P('layer'), may hold values 0 or 1
- widths: int32 [4, 2], P('layer'), may hold values from 256 to 512, as said below
Outputs:
- summed_strips: float32 [4, 768, 3072], P('layer', 'row', 'col')
Inputs may be any that keep to these rules, and one draw needn't show every extreme that they name: `widths`: each supernode uses between half and all of its 512 columns; some supernode uses all. `diag_blocks`: diagonal entries lie between 1 and 4.
All inputs are finite; a program needn't handle non-finite values. No bound on the sum of `block_fill` on one device may be relied on, other than what follows from the above.
Results may differ from a plain program's by a relative error of at most 0.0014.
Values may be sent and summed in bfloat16 or wider, within the bound.
A program may use at most 320 MiB of HBM per device.

v0:
```python
import jax
import jax.numpy as jnp
from jax import lax
from jax.sharding import PartitionSpec as P

BLOCK = 128
NS_ITERS = 3


def partner(block, axis, stride):
    count = lax.axis_size(axis)
    route = []
    for low in range(count):
        high = low | 1 << stride
        if high != low and high < count:
            route += [(low, high), (high, low)]
    return lax.ppermute(block, axis, route)


def masked_system(system_in, width_vec):
    order = system_in.shape[-1]
    indices = jnp.arange(order, dtype=jnp.int32)
    inside = indices[None, :] < width_vec[:, None]
    square = inside[:, :, None] & inside[:, None, :]
    identity = jnp.eye(order, dtype=system_in.dtype)
    return (jnp.where(square, system_in, identity[None]), square)


def on_device(front_copies, lower_panels, upper_panels, diag_blocks, block_fill, widths):
    front = front_copies[0]
    lower = lower_panels[0]
    upper = upper_panels[0]
    system_in = diag_blocks[0]
    fill = block_fill[0]
    width_vec = widths[0]
    row_count = front.shape[0]
    col_count = front.shape[1]
    members = upper.shape[0]
    fill_all = jnp.repeat(fill, BLOCK, axis=1).astype(jnp.float32)
    row_begin = lax.axis_index("row") * row_count
    col_begin = lax.axis_index("col") * col_count
    rows_mask = lax.dynamic_slice_in_dim(fill_all, row_begin, row_count, 1)
    cols_mask = lax.dynamic_slice_in_dim(fill_all, col_begin, col_count, 1)
    system, square = masked_system(system_in, width_vec)
    diagonal = jnp.diagonal(system, axis1=1, axis2=2)
    order = system.shape[-1]
    start_inverse = jnp.eye(order, dtype=jnp.float32)[None] / diagonal[:, None, :]
    inverse = start_inverse
    for sweep_no in range(NS_ITERS):
        product = jnp.einsum("sij,sjk->sik", system, inverse, precision=lax.Precision.HIGHEST)
        inverse = 2.0 * inverse - jnp.einsum(
            "sij,sjk->sik", inverse, product, precision=lax.Precision.HIGHEST
        )
    kept_inverse = jnp.where(square, inverse, 0.0)
    piece = lax.all_gather(upper, "row", axis=1, tiled=True)
    columns = lax.slice_in_dim(kept_inverse, 0, piece.shape[1], axis=2)
    scaled = jnp.zeros((members, order, col_count), jnp.float32) + jnp.einsum(
        "sij,sjk->sik", columns, piece.astype(jnp.float32), precision=lax.Precision.HIGHEST
    )
    scaled_upper = (scaled * cols_mask[:, None, :]).astype(jnp.bfloat16)
    masked_lower = lower * rows_mask[:, :, None].astype(jnp.bfloat16)
    total = jnp.zeros((row_count, col_count), jnp.float32)
    piece = lax.all_gather(masked_lower, "col", axis=2, tiled=True)
    band = lax.slice_in_dim(scaled_upper, 0, piece.shape[2], axis=1)
    for member in range(members):
        total = total + jnp.dot(piece[member], band[member], preferred_element_type=jnp.float32)
    own_copy = front.astype(jnp.float32) - total
    group = min(8, lax.axis_size("layer"))
    levels = group.bit_length() - 1
    strip = row_count // group
    blocks = own_copy.reshape((2,) * levels + (strip, col_count))
    bit_order = list(range(levels))
    axis_bits = list(range(levels - 1, -1, -1))
    layer_index = lax.axis_index("layer")
    for bit_pos in bit_order:
        axis_pos = axis_bits.index(bit_pos)
        upper_side = layer_index >> bit_pos & 1 == 1
        low_half = lax.index_in_dim(blocks, 0, axis_pos, keepdims=False)
        high_half = lax.index_in_dim(blocks, 1, axis_pos, keepdims=False)
        keep_half = jnp.where(upper_side, high_half, low_half)
        send_half = jnp.where(upper_side, low_half, high_half)
        blocks = keep_half + partner(send_half, "layer", bit_pos)
        axis_bits.pop(axis_pos)
    return blocks.reshape(1, strip, col_count)


def solution(mesh):
    placed = (
        P("layer", "row", "col"),
        P("layer", None, "row", "col"),
        P("layer", None, "row", "col"),
        P("layer", None, None, None),
        P("layer", None, None),
        P("layer", None),
    )
    return jax.shard_map(
        on_device, mesh=mesh, in_specs=placed, out_specs=P("layer", "row", "col"), check_vma=False
    )
```

profile of v0, /device:TPU:8, one launch (start us, length us, event | category | flops | bytes accessed | tf_op | source)
XLA Modules:
  0.0 230.0 jit_solution(15805147825050512914)
XLA Ops:
  6.5 0.0 copy-start.5
  6.5 0.0 all-gather.6.cloned.1.call-start
  6.5 0.7 all-gather.6.cloned.1.call-update
  7.3 0.0 all-gather.4.cloned.1.call-start
  7.3 0.7 convert_bitcast_fusion
  8.0 0.1 broadcast_bitcast_fusion
  8.1 2.5 %bitcast_multiply_fusion = bf16[2,1536,128]{2,1,0:T(8,128)(2,1)} fusion(bf16[1,2,1536,128]{3,2,1,0:T(8,128)(2,1)} %param.7, bf16[2,1536]{1,0:T(2,128)(2,1)S(1)} %dynamic-slice_convert_fusion), kind=kLoop, calls=%fused_computation.37 | loop fusion | flops 393216 | bytes 1579008 | tf_op jit(solution)/shard_map/mul | solution.py:61
  10.6 0.0 all-gather.4.cloned.1.call-update
  10.6 0.1 fusion.18
  10.7 0.0 copy-done.5
  10.8 0.1 iota_compare_fusion.1
  10.8 1.9 and_select_fusion.1
  12.7 59.3 %copy.11 = f32[2,512,512]{0,2,1:T(8,128)} copy(f32[2,512,512]{2,1,0:T(8,128)S(1)} %and_select_fusion.1) | data formatting | bytes 4194304 | tf_op jit(solution)/shard_map/jit(_where)/select_n | solution.py:26
  72.1 5.5 %gather_fusion = f32[512,2]{1,0:T(8,128)S(1)} fusion(f32[2,512,512]{0,2,1:T(8,128)} %copy.11, s32[512]{0:T(512)S(1)} %bitcast.69), kind=kCustom, calls=%fused_computation | custom fusion | bytes 12288 | tf_op jit(solution)/shard_map/jit(diagonal)/gather | solution.py:45
  77.6 0.1 copy.12
  77.7 3.6 %fusion.5 = f32[2,512,512]{2,1,0:T(8,128)S(1)} fusion(f32[2,512,512]{2,1,0:T(8,128)S(1)} %and_select_fusion.1, f32[2,512]{1,0:T(2,128)S(1)} %copy.12, f32[512,512]{1,0:T(8,128)S(1)} %fusion.18), kind=kOutput, calls=%fused_computation.16 | convolution fusion | flops 3221749760 | bytes 5246976 | tf_op jit(solution)/shard_map/sij,sjk->sik/dot_general | solution.py:50
  81.3 3.7 %multiply_subtract_fusion.1 = f32[2,512,512]{2,1,0:T(8,128)S(1)} fusion(f32[2,512,512]{2,1,0:T(8,128)S(1)} %fusion.5, f32[2,512]{1,0:T(2,128)S(1)} %copy.12, f32[512,512]{1,0:T(8,128)S(1)} %fusion.18), kind=kOutput, calls=%fused_computation.13 | convolution fusion | flops 3223322624 | bytes 5246976 | tf_op jit(solution)/shard_map/sij,sjk->sik/dot_general | solution.py:51
  85.0 3.6 %fusion.23 = f32[2,512,512]{2,1,0:T(8,128)S(1)} fusion(f32[2,512,512]{2,1,0:T(8,128)S(1)} %and_select_fusion.1, f32[2,512,512]{2,1,0:T(8,128)S(1)} %multiply_subtract_fusion.1), kind=kOutput, calls=%fused_computation.47 | convolution fusion | flops 3221225472 | bytes 6291456 | tf_op jit(solution)/shard_map/sij,sjk->sik/dot_general | solution.py:50
  88.6 3.8 %multiply_subtract_fusion = f32[2,512,512]{2,1,0:T(8,128)S(1)} fusion(f32[2,512,512]{2,1,0:T(8,128)S(1)} %multiply_subtract_fusion.1, f32[2,512,512]{2,1,0:T(8,128)S(1)} %fusion.23), kind=kOutput, calls=%fused_computation.12 | convolution fusion | flops 3222274048 | bytes 6291456 | tf_op jit(solution)/shard_map/sij,sjk->sik/dot_general | solution.py:51
  92.4 0.0 copy-start.1
  92.4 3.5 %fusion.24 = f32[2,512,512]{2,1,0:T(8,128)S(1)} fusion(f32[2,512,512]{2,1,0:T(8,128)S(1)} %and_select_fusion.1, f32[2,512,512]{2,1,0:T(8,128)S(1)} %multiply_subtract_fusion), kind=kOutput, calls=%fused_computation.48 | convolution fusion | flops 3221225472 | bytes 6291456 | tf_op jit(solution)/shard_map/sij,sjk->sik/dot_general | solution.py:50
  96.0 0.0 copy-done.1
  96.0 3.5 %fusion.25 = f32[2,512,512]{2,1,0:T(8,128)S(1)} fusion(f32[2,512,512]{2,1,0:T(8,128)S(1)} %multiply_subtract_fusion, f32[2,512,512]{2,1,0:T(8,128)S(1)} %fusion.24), kind=kOutput, calls=%fused_computation.49 | convolution fusion | flops 3221225472 | bytes 6291456 | tf_op jit(solution)/shard_map/sij,sjk->sik/dot_general | solution.py:51
  99.5 0.0 all-gather.6.cloned.1.call-done
  99.6 6.1 %multiply_convert_fusion = bf16[2,512,768]{2,1,0:T(8,128)(2,1)} fusion(f32[2,512,512]{2,1,0:T(8,128)S(1)} %fusion.25, f32[2,512,512]{2,1,0:T(8,128)} %copy-done.1, bf16[1,2,512,768]{3,2,1,0:T(8,128)(2,1)} %all-gather.6.cloned.1.call-done, f32[2,768]{1,0:T(2,128)S(1)} %constant_dynamic-slice_fusion, pred[2,512]{1,0:T(4,128)(4,1)S(1)} %iota_compare_fusion.1), kind=kOutput, calls=%fused_computation.2 | convolution fusion | flops 4835508224 | bytes 7347200 | tf_op jit(solution)/shard_map/sij,sjk->sik/dot_general | solution.py:57
  105.6 0.0 copy-start.2
  105.6 0.0 all-gather.4.cloned.1.call-done
  105.6 0.0 copy-start.3
  105.7 0.0 copy-start.4
  105.7 3.1 %fusion.7 = f32[1536,768]{1,0:T(8,128)S(1)} fusion(bf16[2,1536,512]{2,1,0:T(8,128)(2,1)} %all-gather.4.cloned.1.call-done, bf16[2,512,768]{2,1,0:T(8,128)(2,1)} %multiply_convert_fusion), kind=kOutput, calls=%fused_computation.20 | convolution fusion | flops 1207959552 | bytes 7077888 | tf_op jit(solution)/shard_map/dot_general | solution.py:66
  108.8 0.0 copy-done.2
  108.8 0.0 copy-done.3
  108.8 0.6 copy-done.4
  109.5 1.4 convert_subtract_fusion
  110.8 0.0 copy-start
  110.9 0.3 select_bitcast_fusion
  111.2 1.8 copy-done
  113.0 0.0 collective-permute-start
  113.0 53.1 %collective-permute-done = f32[2,384,768]{2,1,0:T(8,128)} collective-permute-done((f32[2,384,768]{2,1,0:T(8,128)S(1)}, f32[2,384,768]{2,1,0:T(8,128)}, u32[]{:S(2)}, u32[]{:S(2)}) %collective-permute-start) | collective-permute-done | bytes 2359328 | tf_op jit(solution)/shard_map/ppermute | solution.py:17
  166.1 3.5 %bitcast_add_fusion = f32[2,384,768]{2,1,0:T(8,128)S(1)} fusion(f32[2,384,768]{2,1,0:T(8,128)} %collective-permute-done, f32[2,2,384,768]{3,2,1,0:T(8,128)} %bitcast.68, pred[]{:T(512)S(6)} %eq.17), kind=kLoop, calls=%fused_computation.7 | loop fusion | flops 1179648 | bytes 9437185 | tf_op jit(solution)/shard_map/add | solution.py:82
  169.6 0.1 select_bitcast_fusion.1
  169.8 2.7 %collective-permute-start.1 = (f32[384,768]{1,0:T(8,128)S(1)}, f32[384,768]{1,0:T(8,128)S(1)}, u32[]{:S(2)}, u32[]{:S(2)}) collective-permute-start(f32[384,768]{1,0:T(8,128)S(1)} %select_bitcast_fusion.1), channel_id=1, source_target_pairs={{0,16},{16,0},{8,24},{24,8},{1,17},{17,1},{9,25},{25,9},{2,18},{18... | collective-permute-start | bytes 3538952 | tf_op jit(solution)/shard_map/ppermute | solution.py:17
  172.4 49.5 %collective-permute-done.1 = f32[384,768]{1,0:T(8,128)S(1)} collective-permute-done((f32[384,768]{1,0:T(8,128)S(1)}, f32[384,768]{1,0:T(8,128)S(1)}, u32[]{:S(2)}, u32[]{:S(2)}) %collective-permute-start.1) | collective-permute-done | bytes 1179680 | tf_op jit(solution)/shard_map/ppermute | solution.py:17
  222.0 1.2 fusion.11
  (4 shorter events, 0.0 us)
Async XLA Ops:
  6.5 4.2 %copy-start.5 = (s32[1,2]{1,0:T(1,128)S(1)}, s32[1,2]{1,0:T(1,128)}, u32[]{:S(2)}) copy-start(s32[1,2]{1,0:T(1,128)} %param.11) | copy-start | bytes 28
  6.5 93.0 %all-gather.6.cloned.1.call-start = ((), (), s32[]{:S(2)}) async-start(), calls=%async_computation.1 | async-start | bytes 2359296 | tf_op jit(solution)/shard_map/all_gather | solution.py:55
  7.3 98.4 %all-gather.4.cloned.1.call-start = ((), (), s32[]{:S(2)}) async-start(), calls=%async_computation | async-start | bytes 3932160 | tf_op jit(solution)/shard_map/all_gather | solution.py:63
  92.4 3.6 %copy-start.1 = (f32[2,512,512]{2,1,0:T(8,128)}, f32[2,512,512]{2,1,0:T(8,128)S(1)}, u32[]{:S(2)}) copy-start(f32[2,512,512]{2,1,0:T(8,128)S(1)} %multiply_subtract_fusion) | copy-start | bytes 6291460
  105.6 3.2 %copy-start.2 = (bf16[2,512,768]{2,1,0:T(8,128)(2,1)S(1)}, bf16[2,512,768]{2,1,0:T(8,128)(2,1)}, u32[]{:S(2)}) copy-start(bf16[2,512,768]{2,1,0:T(8,128)(2,1)} %multiply_convert_fusion) | copy-start | bytes 4718596
  105.6 3.2 %copy-start.3 = (bf16[2,1536,512]{2,1,0:T(8,128)(2,1)S(1)}, bf16[2,1536,512]{2,1,0:T(8,128)(2,1)}, u32[]{:S(2)}) copy-start(bf16[2,1536,512]{2,1,0:T(8,128)(2,1)} %all-gather.4.cloned.1.call-done) | copy-start | bytes 9437188
  105.7 3.8 %copy-start.4 = (bf16[1,1536,768]{2,1,0:T(8,128)(2,1)S(1)}, bf16[1,1536,768]{2,1,0:T(8,128)(2,1)}, u32[]{:S(2)}) copy-start(bf16[1,1536,768]{2,1,0:T(8,128)(2,1)} %param.6) | copy-start | bytes 7077892
  110.8 2.1 copy-start
  113.0 53.1 %collective-permute-start = (f32[2,384,768]{2,1,0:T(8,128)S(1)}, f32[2,384,768]{2,1,0:T(8,128)}, u32[]{:S(2)}, u32[]{:S(2)}) collective-permute-start(f32[2,384,768]{2,1,0:T(8,128)S(1)} %select_bitcast_fusion), channel_id=1, source_target_pairs={{0,8},{8,0},{16,24},{24,16},{1,9},{9,1},{17,25},{25,17},{2,10},{10... | collective-permute-start | bytes 7077896 | tf_op jit(solution)/shard_map/ppermute | solution.py:17
  169.8 52.2 %collective-permute-start.1 = (f32[384,768]{1,0:T(8,128)S(1)}, f32[384,768]{1,0:T(8,128)S(1)}, u32[]{:S(2)}, u32[]{:S(2)}) collective-permute-start(f32[384,768]{1,0:T(8,128)S(1)} %select_bitcast_fusion.1), channel_id=1, source_target_pairs={{0,16},{16,0},{8,24},{24,8},{1,17},{17,1},{9,25},{25,9},{2,18},{18... | collective-permute-start | bytes 3538952 | tf_op jit(solution)/shard_map/ppermute | solution.py:17
Sparse Core Ops, SparseCore 0:
  8.9 28.3 all-gather.5
  38.9 28.9 all-gather.3
where the time goes:
time: 233 us; the launch traced here: 230 us
  waiting for transfers between devices  103 us (44%)
  local copies, waits for them, and re-layouts  67.5 us (29%)
  matrix products  32.4 us (14%)
  between operations  13.6 us (6%)
  other arithmetic  10.5 us (5%)
  starting transfers between devices  2.69 us (1%)
    ppermute x2, waiting for transfers between devices, partner(): return lax.ppermute(block, axis, route)  103 us
    select_n x1, local copies, waits for them, and re-layouts, masked_system(): return (jnp.where(square, system_in, identity[None]), square)  59.3 us
    dot_general x3, matrix products, on_device(): jnp.einsum('sij,sjk->sik', inverse, product, precision=lax.Precision.HIGH...  11 us
    dot_general x3, matrix products, on_device(): jnp.einsum('sij,sjk->sik', system, inverse, precision=lax.Precision.HIGHEST)  10.7 us
    dot_general x1, matrix products, on_device(): jnp.einsum('sij,sjk->sik', columns, piece.astype(jnp.float32), precision=...  6.08 us
    gather x2, local copies, waits for them, and re-layouts, on_device(): diagonal = jnp.diagonal(system, axis1=1, axis2=2)  5.59 us
  transfers between devices with their start and end apart: 4, of which 2 were waited for; matrix products, arithmetic and copies ran while one was open for 43% of the time, Pallas kernels for 0%

commit v1 on v0

v1 whole, which is shorter than its diff:
```python
import functools

import jax
import jax.numpy as jnp
from jax import lax
from jax.experimental import pallas as pl
from jax.experimental.pallas import tpu as pltpu
from jax.sharding import PartitionSpec as P

BLOCK = 128
MESH = pl.DeviceIdType.MESH
CHUNK = 256
HEAD = 16


def pack(values, ref):
    rows, cols = values.shape
    top = jnp.maximum(jnp.max(jnp.abs(values), axis=0, keepdims=True), 1e-30)
    power = jnp.ceil(jnp.log2(top))
    coded = jnp.round(values * jnp.exp2(14.0 - power))
    ref[:HEAD, :] = jnp.broadcast_to(power, (HEAD, cols)).astype(jnp.int32).astype(jnp.int16)
    ref[HEAD:, :] = coded.astype(jnp.int32).astype(jnp.int16)


def unpack(ref):
    power = ref[:HEAD, :].astype(jnp.int32).astype(jnp.float32)[:1, :]
    coded = ref[HEAD:, :].astype(jnp.int32).astype(jnp.float32)
    return coded * jnp.exp2(power - 14.0)


def chain_kernel(n, strip, chunks, front, lower, upper, out, send, recv, send_sem, recv_sem):
    layer = lax.axis_index("layer")
    place = lax.rem(layer, n)
    base = layer - place
    has_left = place > 0
    has_right = place < n - 1
    barrier = pltpu.get_barrier_semaphore()

    @pl.when(has_left)
    def _():
        pl.semaphore_signal(barrier, inc=1, device_id={"layer": layer - 1}, device_id_type=MESH)

    @pl.when(has_right)
    def _():
        pl.semaphore_signal(barrier, inc=1, device_id={"layer": layer + 1}, device_id_type=MESH)

    pl.semaphore_wait(barrier, jnp.where(has_left, 1, 0) + jnp.where(has_right, 1, 0))

    members = lower.shape[0]

    def product(t, j):
        rows = pl.ds(pl.multiple_of(t * strip, strip), strip)
        cols = pl.ds(pl.multiple_of(j * CHUNK, CHUNK), CHUNK)
        total = front[rows, cols].astype(jnp.float32)
        for s in range(members):
            total = total - jnp.dot(
                lower[s, rows, :], upper[s, :, cols], preferred_element_type=jnp.float32
            )
        return total

    def copy(way, k, j, target):
        return pltpu.make_async_remote_copy(
            src_ref=send.at[way, k, j],
            dst_ref=recv.at[way, k, j],
            send_sem=send_sem.at[way, k, j],
            recv_sem=recv_sem.at[way, k, j],
            device_id={"layer": target},
            device_id_type=MESH,
        )

    first = jnp.where(place * 2 < n, 0, 1)

    def item(i, _):
        k, rest = i // (2 * chunks), i % (2 * chunks)
        j, turn = rest // 2, rest % 2
        way = jnp.where(turn == 0, first, 1 - first)
        t = jnp.where(way == 0, n - 1 - k, k)
        count = jnp.where(way == 0, n - 1 - place, place)
        fed = jnp.where(way == 0, place, n - 1 - place) > 0
        target = jnp.where(way == 0, layer + 1, layer - 1)
        source = jnp.where(way == 0, layer - 1, layer + 1)

        @pl.when(k < count)
        def _():
            value = product(t, j)
            slot = send.at[way, k, j]

            @pl.when(fed)
            def _():
                copy(way, k, j, source).wait_recv()
                pack(value + unpack(recv.at[way, k, j]), slot)

            @pl.when(jnp.logical_not(fed))
            def _():
                pack(value, slot)

            copy(way, k, j, target).start()

        return 0

    lax.fori_loop(0, (n - 1) * chunks * 2, item, 0)

    def own(j, _):
        cols = pl.ds(pl.multiple_of(j * CHUNK, CHUNK), CHUNK)
        out[0, :, cols] = product(place, j)
        return 0

    lax.fori_loop(0, chunks, own, 0)

    def finish(j, _):
        cols = pl.ds(pl.multiple_of(j * CHUNK, CHUNK), CHUNK)
        for turn in range(2):
            way = first if turn == 0 else 1 - first
            way = 1 - way
            k = jnp.where(way == 0, n - 1 - place, place)
            fed = jnp.where(way == 0, place, n - 1 - place) > 0
            source = jnp.where(way == 0, layer - 1, layer + 1)

            @pl.when(fed)
            def _():
                copy(way, k, j, source).wait_recv()
                out[0, :, cols] = out[0, :, cols] + unpack(recv.at[way, k, j])

        return 0

    lax.fori_loop(0, chunks, finish, 0)

    def drain(i, _):
        k, rest = i // (2 * chunks), i % (2 * chunks)
        j, way = rest // 2, rest % 2
        count = jnp.where(way == 0, n - 1 - place, place)
        target = jnp.where(way == 0, layer + 1, layer - 1)

        @pl.when(k < count)
        def _():
            copy(way, k, j, target).wait_send()

        return 0

    lax.fori_loop(0, (n - 1) * chunks * 2, drain, 0)


def update_and_sum(front, lower, upper, n):
    rows, cols = front.shape
    strip = rows // n
    chunks = cols // CHUNK
    return pl.pallas_call(
        functools.partial(chain_kernel, n, strip, chunks),
        out_shape=jax.ShapeDtypeStruct((1, strip, cols), jnp.float32),
        in_specs=[pl.BlockSpec(memory_space=pltpu.VMEM)] * 3,
        out_specs=pl.BlockSpec(memory_space=pltpu.VMEM),
        scratch_shapes=[
            pltpu.VMEM((2, n - 1, chunks, strip + HEAD, CHUNK), jnp.int16),
            pltpu.VMEM((2, n - 1, chunks, strip + HEAD, CHUNK), jnp.int16),
            pltpu.SemaphoreType.DMA((2, n - 1, chunks)),
            pltpu.SemaphoreType.DMA((2, n - 1, chunks)),
        ],
        compiler_params=pltpu.CompilerParams(
            collective_id=0, has_side_effects=True, vmem_limit_bytes=48 * 2**20
        ),
    )(front, lower, upper)


def kept_inverses(system_in, width_vec):
    order = system_in.shape[-1]
    indices = jnp.arange(order, dtype=jnp.int32)
    inside = indices[None, :] < width_vec[:, None]
    square = inside[:, :, None] & inside[:, None, :]
    eye = jnp.eye(order, dtype=jnp.float32)[None]
    system = jnp.where(square, system_in, eye)
    start = 1.0 / jnp.sum(system * eye, axis=2)
    inverse = 2.0 * eye * start[:, None, :] - start[:, :, None] * system * start[:, None, :]
    for _ in range(2):
        product = jnp.einsum("sij,sjk->sik", system, inverse, precision=lax.Precision.HIGH)
        inverse = 2.0 * inverse - jnp.einsum(
            "sij,sjk->sik", inverse, product, precision=lax.Precision.HIGH
        )
    return jnp.where(square, inverse, 0.0)


def on_device(front_copies, lower_panels, upper_panels, diag_blocks, block_fill, widths):
    front = front_copies[0]
    upper = upper_panels[0]
    row_count, col_count = front.shape
    fill_all = jnp.repeat(block_fill[0], BLOCK, axis=1).astype(jnp.float32)
    rows_mask = lax.dynamic_slice_in_dim(fill_all, lax.axis_index("row") * row_count, row_count, 1)
    cols_mask = lax.dynamic_slice_in_dim(fill_all, lax.axis_index("col") * col_count, col_count, 1)
    lower = lower_panels[0] * rows_mask[:, :, None].astype(jnp.bfloat16)
    lower = lax.all_gather(lower, "col", axis=2, tiled=True)
    upper = lax.all_gather(upper, "row", axis=1, tiled=True)
    inverse = kept_inverses(diag_blocks[0], widths[0])
    scaled = jnp.einsum(
        "sij,sjk->sik", inverse, upper.astype(jnp.float32), precision=lax.Precision.HIGH
    )
    scaled = (scaled * cols_mask[:, None, :]).astype(jnp.bfloat16)
    group = min(8, lax.axis_size("layer"))
    return update_and_sum(front, lower, scaled, group)


def solution(mesh):
    placed = (
        P("layer", "row", "col"),
        P("layer", None, "row", "col"),
        P("layer", None, "row", "col"),
        P("layer", None, None, None),
        P("layer", None, None),
        P("layer", None),
    )
    return jax.shard_map(
        on_device, mesh=mesh, in_specs=placed, out_specs=P("layer", "row", "col"), check_vma=False
    )
```

time: 233 us -> 123 us (0.53); the launches traced: 230 us -> 123 us
  local copies, waits for them, and re-layouts: 67.5 us -> 2.81 us
  waiting for transfers between devices: 103 us -> 41.6 us
  Pallas kernels: 0 us -> 45.5 us
  matrix products: 32.4 us -> 15.1 us
  other arithmetic: 10.5 us -> 4.26 us
  starting transfers between devices: 2.69 us -> 0.04 us
    ppermute x2 -> x0, waiting for transfers between devices: 103 us -> none  [partner(): return lax.ppermute(block, axis, route)]
    select_n x1 -> x0, local copies, waits for them, and re-layouts: 59.3 us -> none  [masked_system(): return (jnp.where(square, system_in, identity[None]), square)]
    pallas_call x0 -> x1, Pallas kernels: none -> 45.5 us  [update_and_sum(): pl.pallas_call(functools.partial(chain_kernel, n, strip, chunks), out_sha...]
    all_gather x2, waiting for transfers between devices: 0.02 us -> 40.8 us  [the longest x1 26 us: on_device(): lower = lax.all_gather(lower, 'col', axis=2, tiled=True)]
    dot_general x9 -> x5, matrix products: 32.4 us -> 15.1 us  [the longest x2 6.07 us: kept_inverses(): jnp.einsum('sij,sjk->sik', inverse, product, precision=lax.Precision.HIGH)]
    gather x2 -> x0, local copies, waits for them, and re-layouts: 5.59 us -> none  [on_device(): diagonal = jnp.diagonal(system, axis1=1, axis2=2)]
    add x1 -> x0, other arithmetic: 3.54 us -> none  [on_device(): blocks = keep_half + partner(send_half, 'layer', bit_pos)]
    ppermute x2 -> x0, starting transfers between devices: 2.65 us -> none  [partner(): return lax.ppermute(block, axis, route)]
  transfers between devices with their start and end apart: 4 -> 2, of which waited for: 2 -> 2; matrix products, arithmetic and copies ran while one was open for 43% -> 16% of each run, Pallas kernels for 0% -> 0%
where the time goes in v1:
time: 123 us
  Pallas kernels  45.5 us (37%)
  waiting for transfers between devices  41.6 us (34%)
  matrix products  15.1 us (12%)
  between operations  13.5 us (11%)
  other arithmetic  4.26 us (3%)
  local copies, waits for them, and re-layouts  2.81 us (2%)
    pallas_call x1, Pallas kernels, update_and_sum(): pl.pallas_call(functools.partial(chain_kernel, n, strip, chunks), out_sha...  45.5 us
    all_gather x1, waiting for transfers between devices, on_device(): lower = lax.all_gather(lower, 'col', axis=2, tiled=True)  26 us
    all_gather x1, waiting for transfers between devices, on_device(): upper = lax.all_gather(upper, 'row', axis=1, tiled=True)  14.9 us
    dot_general x2, matrix products, kept_inverses(): jnp.einsum('sij,sjk->sik', inverse, product, precision=lax.Precision.HIGH)  6.07 us
    dot_general x2, matrix products, kept_inverses(): jnp.einsum('sij,sjk->sik', system, inverse, precision=lax.Precision.HIGH)  4.55 us
    dot_general x1, matrix products, on_device(): jnp.einsum('sij,sjk->sik', inverse, upper.astype(jnp.float32), precision=...  4.54 us
    unnamed x11, local copies, waits for them, and re-layouts  2.79 us
    mul x1, other arithmetic, on_device(): lower = lower_panels[0] * rows_mask[:, :, None].astype(jnp.bfloat16)  2.64 us
  transfers between devices with their start and end apart: 2, of which 2 were waited for; matrix products, arithmetic and copies ran while one was open for 16% of the time, Pallas kernels for 0%

profile of v1, /device:TPU:8, one launch (start us, length us, event | category | flops | bytes accessed | tf_op | source)
XLA Modules:
  0.0 122.8 jit_solution(5047769812591411062)
XLA Ops:
  6.5 0.0 all-gather.6.cloned.1.call-start
  6.5 0.7 all-gather.6.cloned.1.call-update
  7.3 0.0 all-gather.4.cloned.1.call-start
  7.3 0.7 convert_bitcast_fusion
  8.0 0.1 broadcast_bitcast_fusion
  8.1 0.0 copy-start.3
  8.1 0.0 copy-start.1
  8.1 2.6 %bitcast_multiply_fusion = bf16[2,1536,128]{2,1,0:T(8,128)(2,1)} fusion(bf16[1,2,1536,128]{3,2,1,0:T(8,128)(2,1)} %param.7, bf16[2,1536]{1,0:T(2,128)(2,1)S(1)} %dynamic-slice_convert_fusion), kind=kLoop, calls=%fused_computation.35 | loop fusion | flops 393216 | bytes 1579008 | tf_op jit(solution)/shard_map/mul | solution.py:188
  10.8 0.0 all-gather.4.cloned.1.call-update
  10.8 0.1 fusion.18
  10.9 0.1 fusion.19
  11.1 0.0 copy-done.3
  11.1 0.1 iota_compare_fusion.1
  11.1 0.0 copy-done.1
  11.1 0.6 multiply_reduce_fusion
  11.8 2.6 %fusion.4 = f32[2,512,512]{2,1,0:T(8,128)S(1)} fusion(f32[1,2,512,512]{3,2,1,0:T(8,128)S(1)} %copy-done.1, f32[2,512]{1,0:T(2,128)S(1)} %broadcast_divide_fusion, f32[512,512]{1,0:T(8,128)S(1)} %fusion.18, f32[512,512]{1,0:T(8,128)S(1)} %fusion.19, pred[2,512]{1,0:T(4,128)(4,1)S(1)} %iota_compare_fusion.1), kind=kOutput, calls=%fused_computation.9 | convolution fusion | flops 1614807040 | bytes 6296576 | tf_op jit(solution)/shard_map/sij,sjk->sik/dot_general | solution.py:174
  14.4 2.8 %multiply_subtract_fusion = f32[2,512,512]{2,1,0:T(8,128)S(1)} fusion(f32[2,512,512]{2,1,0:T(8,128)S(1)} %fusion.4, f32[1,2,512,512]{3,2,1,0:T(8,128)S(1)} %copy-done.1, f32[2,512]{1,0:T(2,128)S(1)} %broadcast_divide_fusion, f32[512,512]{1,0:T(8,128)S(1)} %fusion.18, f32[512,512]{1,0:T(8,128)S(1)} %fusion.19, pred[2,512]{1,0:T(4,128)(4,1)S(1)} %iota_compare_fusion.1), kind=kOutput, calls=%fused_computation.6 | convolution fusion | flops 1617952768 | bytes 8393728 | tf_op jit(solution)/shard_map/sij,sjk->sik/dot_general | solution.py:175
  17.1 0.0 copy-start.2
  17.1 2.0 %fusion.6 = f32[2,512,512]{2,1,0:T(8,128)S(1)} fusion(f32[2,512,512]{2,1,0:T(8,128)S(1)} %multiply_subtract_fusion, f32[1,2,512,512]{3,2,1,0:T(8,128)S(1)} %copy-done.1, f32[512,512]{1,0:T(8,128)S(1)} %fusion.18, pred[2,512]{1,0:T(4,128)(4,1)S(1)} %iota_compare_fusion.1), kind=kOutput, calls=%fused_computation.12 | convolution fusion | flops 1611661312 | bytes 7341056 | tf_op jit(solution)/shard_map/sij,sjk->sik/dot_general | solution.py:174
  19.1 0.0 copy-done.2
  19.1 3.3 %fusion.30 = f32[2,512,512]{2,1,0:T(8,128)} fusion(f32[2,512,512]{2,1,0:T(8,128)S(1)} %multiply_subtract_fusion, f32[2,512,512]{2,1,0:T(8,128)S(1)} %fusion.6), kind=kOutput, calls=%fused_computation.45 | convolution fusion | flops 1610612736 | bytes 6291456 | tf_op jit(solution)/shard_map/sij,sjk->sik/dot_general | solution.py:175
  22.4 14.9 %all-gather.6.cloned.1.call-done = bf16[1,2,512,768]{3,2,1,0:T(8,128)(2,1)} async-done(((bf16[1,2,256,768]{3,2,1,0:T(8,128)(2,1)}), bf16[1,2,512,768]{3,2,1,0:T(8,128)(2,1)}) %all-gather.6.cloned.1.call-update) | async-done | bytes 1572880 | tf_op jit(solution)/shard_map/all_gather | solution.py:190
  37.3 4.5 %multiply_convert_fusion.upper = bf16[2,512,768]{2,1,0:T(8,128)(2,1)S(1)} fusion(f32[2,512,512]{2,1,0:T(8,128)} %fusion.30, f32[2,512,512]{2,1,0:T(8,128)} %copy-done.2, bf16[1,2,512,768]{3,2,1,0:T(8,128)(2,1)} %all-gather.6.cloned.1.call-done, f32[2,768]{1,0:T(2,128)S(1)} %constant_dynamic-slice_fusion, pred[2,512]{1,0:T(4,128)(4,1)S(1)} %iota_compare_fusion.1), kind=kOutput, calls=%fused_computation | convolution fusion | flops 2419589120 | bytes 7347200 | tf_op jit(solution)/shard_map/sij,sjk->sik/dot_general | solution.py:192
  41.9 26.0 %all-gather.4.cloned.1.call-done.lower = bf16[2,1536,512]{2,1,0:T(8,128)(2,1)} async-done(((bf16[2,1536,128]{2,1,0:T(8,128)(2,1)}), bf16[2,1536,512]{2,1,0:T(8,128)(2,1)}) %all-gather.4.cloned.1.call-update) | async-done | bytes 3145744 | tf_op jit(solution)/shard_map/all_gather | solution.py:189
  67.8 0.0 copy-start
  67.8 1.7 %copy-done = bf16[1,1536,768]{2,1,0:T(8,128)(2,1)S(1)} copy-done((bf16[1,1536,768]{2,1,0:T(8,128)(2,1)S(1)}, bf16[1,1536,768]{2,1,0:T(8,128)(2,1)}, u32[]{:S(2)}) %copy-start) | copy-done | bytes 2359320
  69.5 45.5 %shard_map.64 = f32[1,384,768]{2,1,0:T(8,128)S(1)} custom-call(bf16[1536,768]{1,0:T(8,128)(2,1)S(1)} %bitcast.32, bf16[2,1536,512]{2,1,0:T(8,128)(2,1)} %all-gather.4.cloned.1.call-done.lower, bf16[2,512,768]{2,1,0:T(8,128)(2,1)S(1)} %multiply_convert_fusion.upper), custom_call_target="tpu_custom_call" | custom-call | tf_op jit(solution)/shard_map/pallas_call | solution.py:147
  115.0 1.0 copy.11
  (4 shorter events, 0.0 us)
Async XLA Ops:
  6.5 30.8 %all-gather.6.cloned.1.call-start = ((), (), s32[]{:S(2)}) async-start(), calls=%async_computation.1 | async-start | bytes 2359296 | tf_op jit(solution)/shard_map/all_gather | solution.py:190
  7.3 60.6 %all-gather.4.cloned.1.call-start = ((), (), s32[]{:S(2)}) async-start(), calls=%async_computation | async-start | bytes 3932160 | tf_op jit(solution)/shard_map/all_gather | solution.py:189
  8.1 2.9 %copy-start.3 = (s32[1,2]{1,0:T(1,128)S(1)}, s32[1,2]{1,0:T(1,128)}, u32[]{:S(2)}) copy-start(s32[1,2]{1,0:T(1,128)} %param.11) | copy-start | bytes 28
  8.1 3.0 %copy-start.1 = (f32[1,2,512,512]{3,2,1,0:T(8,128)S(1)}, f32[1,2,512,512]{3,2,1,0:T(8,128)}, u32[]{:S(2)}) copy-start(f32[1,2,512,512]{3,2,1,0:T(8,128)} %param.9) | copy-start | bytes 6291460
  17.1 2.0 %copy-start.2 = (f32[2,512,512]{2,1,0:T(8,128)}, f32[2,512,512]{2,1,0:T(8,128)S(1)}, u32[]{:S(2)}) copy-start(f32[2,512,512]{2,1,0:T(8,128)S(1)} %multiply_subtract_fusion) | copy-start | bytes 6291460
  67.8 1.7 %copy-start = (bf16[1,1536,768]{2,1,0:T(8,128)(2,1)S(1)}, bf16[1,1536,768]{2,1,0:T(8,128)(2,1)}, u32[]{:S(2)}) copy-start(bf16[1,1536,768]{2,1,0:T(8,128)(2,1)} %param.6) | copy-start | bytes 7077892
Sparse Core Ops, SparseCore 0:
  8.9 28.3 all-gather.5
  38.9 28.9 all-gather.3

commit v2 on v1

--- a/solution.py
+++ b/solution.py
@@ -28,12 +28,89 @@
     return coded * jnp.exp2(power - 14.0)
 
 
-def chain_kernel(n, strip, chunks, front, lower, upper, out, send, recv, send_sem, recv_sem):
+def split(values):
+    high = values.astype(jnp.bfloat16)
+    return high, (values - high.astype(jnp.float32)).astype(jnp.bfloat16)
+
+
+def dot(a, b):
+    return jnp.dot(a, b, preferred_element_type=jnp.float32)
+
+
+def dot_split(a, b):
+    return dot(a[0], b[0]) + (dot(a[0], b[1]) + dot(a[1], b[0]))
+
+
+def inverse_of(block, width):
+    rows = lax.broadcasted_iota(jnp.int32, block.shape, 0)
+    cols = lax.broadcasted_iota(jnp.int32, block.shape, 1)
+    square = (rows < width) & (cols < width)
+    system = jnp.where(square, block, jnp.where(rows == cols, 1.0, 0.0))
+    diagonal = jnp.where(rows == cols, system, 0.0)
+    start_rows = 1.0 / jnp.sum(diagonal, axis=1, keepdims=True)
+    start_cols = 1.0 / jnp.sum(diagonal, axis=0, keepdims=True)
+    inverse = jnp.where(rows == cols, 2.0 * start_cols, 0.0) - start_rows * system * start_cols
+    system = split(system)
+    for _ in range(2):
+        halves = split(inverse)
+        product = split(dot_split(system, halves))
+        inverse = 2.0 * inverse - dot_split(halves, product)
+    return jnp.where(square, inverse, 0.0)
+
+
+def front_kernel(
+    n, n_col, n_row, strip, chunks,
+    front_in, lower_in, upper_in, diag_in, fill, widths, out,
+    front, lower_own, lower, upper, scaled, diag, inv, send, recv,
+    load_sem, lower_send, lower_recv, upper_send, upper_recv, upper_load,
+    inv_send, inv_recv, send_sem, recv_sem,
+):
     layer = lax.axis_index("layer")
+    col = lax.axis_index("col")
+    row = lax.axis_index("row")
     place = lax.rem(layer, n)
-    base = layer - place
     has_left = place > 0
     has_right = place < n - 1
+    members, row_count, width = lower_own.shape
+    part = upper_in.shape[2]
+    half = lax.rem(col, 2)
+    mate = col + 1 - 2 * half
+
+    front_load = pltpu.make_async_copy(front_in.at[0], front, load_sem.at[0])
+    lower_load = pltpu.make_async_copy(lower_in.at[0], lower_own, load_sem.at[1])
+    diag_load = pltpu.make_async_copy(diag_in.at[0, half], diag, load_sem.at[2])
+    lower_load.start()
+    diag_load.start()
+
+    def upper_view(ref_row, j):
+        rows = pl.ds(pl.multiple_of(ref_row * part, part), part)
+        return upper.at[:, rows, pl.ds(pl.multiple_of(j * CHUNK, CHUNK), CHUNK)]
+
+    def upper_copy(d, j):
+        return pltpu.make_async_remote_copy(
+            src_ref=upper_in.at[0, :, :, pl.ds(pl.multiple_of(j * CHUNK, CHUNK), CHUNK)],
+            dst_ref=upper_view(row, j),
+            send_sem=upper_send.at[d - 1, j],
+            recv_sem=upper_recv.at[d - 1, j],
+            device_id={"row": lax.rem(row + d, n_row)},
+            device_id_type=MESH,
+        )
+
+    def upper_arrived(d, j):
+        return pltpu.make_async_remote_copy(
+            src_ref=upper_in.at[0, :, :, pl.ds(pl.multiple_of(j * CHUNK, CHUNK), CHUNK)],
+            dst_ref=upper_view(lax.rem(row + n_row - d, n_row), j),
+            send_sem=upper_send.at[d - 1, j],
+            recv_sem=upper_recv.at[d - 1, j],
+            device_id={"row": lax.rem(row + n_row - d, n_row)},
+            device_id_type=MESH,
+        )
+
+    rows_own = pl.ds(pl.multiple_of(row * part, part), part)
+    upper_own = pltpu.make_async_copy(upper_in.at[0], upper.at[:, rows_own, :], upper_load)
+    upper_own.start()
+    front_load.start()
+
     barrier = pltpu.get_barrier_semaphore()
 
     @pl.when(has_left)
@@ -44,18 +121,113 @@
     def _():
         pl.semaphore_signal(barrier, inc=1, device_id={"layer": layer + 1}, device_id_type=MESH)
 
-    pl.semaphore_wait(barrier, jnp.where(has_left, 1, 0) + jnp.where(has_right, 1, 0))
-
-    members = lower.shape[0]
+    for d in range(1, n_col):
+        pl.semaphore_signal(
+            barrier, inc=1, device_id={"col": lax.rem(col + d, n_col)}, device_id_type=MESH
+        )
+    for d in range(1, n_row):
+        pl.semaphore_signal(
+            barrier, inc=1, device_id={"row": lax.rem(row + d, n_row)}, device_id_type=MESH
+        )
+    near = jnp.where(has_left, 1, 0) + jnp.where(has_right, 1, 0)
+    pl.semaphore_wait(barrier, near + n_col - 1 + n_row - 1)
+
+    for j in range(chunks):
+        for d in range(1, n_row):
+            upper_copy(d, j).start()
+
+    lower_load.wait()
+    own_cols = pl.ds(pl.multiple_of(col * width, width), width)
+    blocks = row_count // BLOCK
+    for s in range(members):
+        for b in range(blocks):
+            flag = fill[0, s, row * blocks + b].astype(jnp.float32)
+            piece = lower_own[s, b * BLOCK : (b + 1) * BLOCK, :].astype(jnp.float32) * flag
+            lower[s, b * BLOCK : (b + 1) * BLOCK, own_cols] = piece.astype(jnp.bfloat16)
+
+    def lower_copy(d, t, sign):
+        peer = lax.rem(col + n_col + sign * d, n_col)
+        source = col if sign > 0 else peer
+        view = lower.at[
+            :,
+            pl.ds(pl.multiple_of(t * strip, strip), strip),
+            pl.ds(pl.multiple_of(source * width, width), width),
+        ]
+        return pltpu.make_async_remote_copy(
+            src_ref=view,
+            dst_ref=view,
+            send_sem=lower_send.at[d - 1, t],
+            recv_sem=lower_recv.at[d - 1, t],
+            device_id={"col": peer},
+            device_id_type=MESH,
+        )
+
+    def send_strip(t):
+        for d in range(1, n_col):
+            lower_copy(d, t, 1).start()
+
+    def send_strips(k, _):
+        @pl.when(k < n - 1 - place)
+        def _():
+            send_strip(n - 1 - k)
+
+        @pl.when(k < place)
+        def _():
+            send_strip(k)
+
+        return 0
+
+    lax.fori_loop(0, n - 1, send_strips, 0)
+    send_strip(place)
+
+    diag_load.wait()
+    high, low = split(inverse_of(diag[...], widths[0, half]))
+    inv[half, 0] = high
+    inv[half, 1] = low
+
+    def inv_copy(m):
+        return pltpu.make_async_remote_copy(
+            src_ref=inv.at[m],
+            dst_ref=inv.at[m],
+            send_sem=inv_send,
+            recv_sem=inv_recv,
+            device_id={"col": mate},
+            device_id_type=MESH,
+        )
+
+    inv_copy(half).start()
+
+    def scale(s, j):
+        cols = pl.ds(pl.multiple_of(j * CHUNK, CHUNK), CHUNK)
+        panel = upper[s, :, cols]
+        value = dot(inv[s, 0], panel) + dot(inv[s, 1], panel)
+        for b in range(CHUNK // BLOCK):
+            flag = fill[0, s, (col * chunks + j) * (CHUNK // BLOCK) + b].astype(jnp.float32)
+            piece = value[:, b * BLOCK : (b + 1) * BLOCK] * flag
+            at = pl.ds(pl.multiple_of(j * CHUNK + b * BLOCK, BLOCK), BLOCK)
+            scaled[s, :, at] = piece.astype(jnp.bfloat16)
+
+    def wait_upper(j):
+        for d in range(1, n_row):
+            upper_arrived(d, j).wait_recv()
+
+    def wait_lower(t):
+        for d in range(1, n_col):
+            lower_copy(d, t, -1).wait_recv()
+
+    upper_own.wait()
+    wait_upper(0)
+    scale(half, 0)
+    inv_copy(1 - half).wait_recv()
+    scale(1 - half, 0)
+    front_load.wait()
 
     def product(t, j):
         rows = pl.ds(pl.multiple_of(t * strip, strip), strip)
         cols = pl.ds(pl.multiple_of(j * CHUNK, CHUNK), CHUNK)
         total = front[rows, cols].astype(jnp.float32)
         for s in range(members):
-            total = total - jnp.dot(
-                lower[s, rows, :], upper[s, :, cols], preferred_element_type=jnp.float32
-            )
+            total = total - dot(lower[s, rows, :], scaled[s, :, cols])
         return total
 
     def copy(way, k, j, target):
@@ -80,6 +252,16 @@
         target = jnp.where(way == 0, layer + 1, layer - 1)
         source = jnp.where(way == 0, layer - 1, layer + 1)
 
+        @pl.when((k == 0) & (j > 0) & (turn == 0))
+        def _():
+            wait_upper(j)
+            for s in range(members):
+                scale(s, j)
+
+        @pl.when((k < count) & (j == 0))
+        def _():
+            wait_lower(t)
+
         @pl.when(k < count)
         def _():
             value = product(t, j)
@@ -99,6 +281,8 @@
         return 0
 
     lax.fori_loop(0, (n - 1) * chunks * 2, item, 0)
+
+    wait_lower(place)
 
     def own(j, _):
         cols = pl.ds(pl.multiple_of(j * CHUNK, CHUNK), CHUNK)
@@ -138,63 +322,59 @@
         return 0
 
     lax.fori_loop(0, (n - 1) * chunks * 2, drain, 0)
-
-
-def update_and_sum(front, lower, upper, n):
-    rows, cols = front.shape
+    inv_copy(half).wait_send()
+    for d in range(1, n_row):
+        for j in range(chunks):
+            upper_copy(d, j).wait_send()
+
+    def drain_lower(t, _):
+        for d in range(1, n_col):
+            lower_copy(d, t, 1).wait_send()
+        return 0
+
+    lax.fori_loop(0, n, drain_lower, 0)
+
+
+def on_device(n, n_col, n_row, front, lower, upper, diag, fill, widths):
+    rows, cols = front.shape[1:]
+    members, part = upper.shape[1:3]
+    width = lower.shape[3]
+    order = diag.shape[2]
     strip = rows // n
     chunks = cols // CHUNK
+    anywhere = pl.BlockSpec(memory_space=pl.ANY)
+    scalars = pl.BlockSpec(memory_space=pltpu.SMEM)
+    dma = pltpu.SemaphoreType.DMA
     return pl.pallas_call(
-        functools.partial(chain_kernel, n, strip, chunks),
+        functools.partial(front_kernel, n, n_col, n_row, strip, chunks),
         out_shape=jax.ShapeDtypeStruct((1, strip, cols), jnp.float32),
-        in_specs=[pl.BlockSpec(memory_space=pltpu.VMEM)] * 3,
+        in_specs=[anywhere] * 4 + [scalars] * 2,
         out_specs=pl.BlockSpec(memory_space=pltpu.VMEM),
         scratch_shapes=[
+            pltpu.VMEM((rows, cols), jnp.bfloat16),
+            pltpu.VMEM((members, rows, width), jnp.bfloat16),
+            pltpu.VMEM((members, rows, order), jnp.bfloat16),
+            pltpu.VMEM((members, order, cols), jnp.bfloat16),
+            pltpu.VMEM((members, order, cols), jnp.bfloat16),
+            pltpu.VMEM((order, order), jnp.float32),
+            pltpu.VMEM((members, 2, order, order), jnp.bfloat16),
             pltpu.VMEM((2, n - 1, chunks, strip + HEAD, CHUNK), jnp.int16),
             pltpu.VMEM((2, n - 1, chunks, strip + HEAD, CHUNK), jnp.int16),
-            pltpu.SemaphoreType.DMA((2, n - 1, chunks)),
-            pltpu.SemaphoreType.DMA((2, n - 1, chunks)),
+            dma((3,)),
+            dma((n_col - 1, n)),
+            dma((n_col - 1, n)),
+            dma((n_row - 1, chunks)),
+            dma((n_row - 1, chunks)),
+            dma,
+            dma,
+            dma,
+            dma((2, n - 1, chunks)),
+            dma((2, n - 1, chunks)),
         ],
         compiler_params=pltpu.CompilerParams(
             collective_id=0, has_side_effects=True, vmem_limit_bytes=48 * 2**20
         ),
-    )(front, lower, upper)
-
-
-def kept_inverses(system_in, width_vec):
-    order = system_in.shape[-1]
-    indices = jnp.arange(order, dtype=jnp.int32)
-    inside = indices[None, :] < width_vec[:, None]
-    square = inside[:, :, None] & inside[:, None, :]
-    eye = jnp.eye(order, dtype=jnp.float32)[None]
-    system = jnp.where(square, system_in, eye)
-    start = 1.0 / jnp.sum(system * eye, axis=2)
-    inverse = 2.0 * eye * start[:, None, :] - start[:, :, None] * system * start[:, None, :]
-    for _ in range(2):
-        product = jnp.einsum("sij,sjk->sik", system, inverse, precision=lax.Precision.HIGH)
-        inverse = 2.0 * inverse - jnp.einsum(
-            "sij,sjk->sik", inverse, product, precision=lax.Precision.HIGH
-        )
-    return jnp.where(square, inverse, 0.0)
-
-
-def on_device(front_copies, lower_panels, upper_panels, diag_blocks, block_fill, widths):
-    front = front_copies[0]
-    upper = upper_panels[0]
-    row_count, col_count = front.shape
-    fill_all = jnp.repeat(block_fill[0], BLOCK, axis=1).astype(jnp.float32)
-    rows_mask = lax.dynamic_slice_in_dim(fill_all, lax.axis_index("row") * row_count, row_count, 1)
-    cols_mask = lax.dynamic_slice_in_dim(fill_all, lax.axis_index("col") * col_count, col_count, 1)
-    lower = lower_panels[0] * rows_mask[:, :, None].astype(jnp.bfloat16)
-    lower = lax.all_gather(lower, "col", axis=2, tiled=True)
-    upper = lax.all_gather(upper, "row", axis=1, tiled=True)
-    inverse = kept_inverses(diag_blocks[0], widths[0])
-    scaled = jnp.einsum(
-        "sij,sjk->sik", inverse, upper.astype(jnp.float32), precision=lax.Precision.HIGH
-    )
-    scaled = (scaled * cols_mask[:, None, :]).astype(jnp.bfloat16)
-    group = min(8, lax.axis_size("layer"))
-    return update_and_sum(front, lower, scaled, group)
+    )(front, lower, upper, diag, fill, widths)
 
 
 def solution(mesh):
@@ -206,6 +386,9 @@
         P("layer", None, None),
         P("layer", None),
     )
+    body = functools.partial(
+        on_device, min(8, mesh.shape["layer"]), mesh.shape["col"], mesh.shape["row"]
+    )
     return jax.shard_map(
-        on_device, mesh=mesh, in_specs=placed, out_specs=P("layer", "row", "col"), check_vma=False
+        body, mesh=mesh, in_specs=placed, out_specs=P("layer", "row", "col"), check_vma=False
     )

time: 123 us -> 63.5 us (0.52)
  waiting for transfers between devices: 41.6 us -> 0 us
  matrix products: 15.1 us -> 0 us
  between operations: 13.5 us -> 0.01 us
  Pallas kernels: 45.5 us -> 57 us
  other arithmetic: 4.26 us -> 0 us
  local copies, waits for them, and re-layouts: 2.81 us -> 6.2 us
    all_gather x2 -> x0, waiting for transfers between devices: 40.8 us -> none  [the longest x1 26 us: on_device(): lower = lax.all_gather(lower, 'col', axis=2, tiled=True)]
    dot_general x5 -> x0, matrix products: 15.1 us -> none  [the longest x2 6.07 us: kept_inverses(): jnp.einsum('sij,sjk->sik', inverse, product, precision=lax.Precision.HIGH)]
    pallas_call x1, Pallas kernels: 45.5 us -> 57 us  [on_device(): pl.pallas_call(functools.partial(front_kernel, n, n_col, n_row, strip, ch...]
    unnamed x11, local copies, waits for them, and re-layouts: 2.79 us -> 6.2 us
    mul x2 -> x0, other arithmetic: 2.75 us -> none  [the longest x1 2.64 us: on_device(): lower = lower_panels[0] * rows_mask[:, :, None].astype(jnp.bfloat16)]
  transfers between devices with their start and end apart: 2 -> 0, of which waited for: 2 -> 0; matrix products, arithmetic and copies ran while one was open for 16% -> 0% of each run, Pallas kernels for 0% -> 0%
where the time goes in v2:
time: 63.5 us; the launch traced here: 63.2 us
  Pallas kernels  57 us (90%)
  local copies, waits for them, and re-layouts  6.2 us (10%)
    pallas_call x1, Pallas kernels, on_device(): pl.pallas_call(functools.partial(front_kernel, n, n_col, n_row, strip, ch...  57 us
    unnamed x11, local copies, waits for them, and re-layouts  6.2 us

profile of v2, /device:TPU:8, one launch (start us, length us, event | category | flops | bytes accessed | tf_op | source)
XLA Modules:
  0.0 63.2 jit_solution(10531106537587310691)
XLA Ops:
  0.0 0.0 copy-start
  0.0 1.6 %copy-done = f32[1,2,512,512]{3,2,1,0:T(8,128)S(1)} copy-done((f32[1,2,512,512]{3,2,1,0:T(8,128)S(1)}, f32[1,2,512,512]{3,2,1,0:T(8,128)}, u32[]{:S(2)}) %copy-start) | copy-done | bytes 2097176
  1.6 0.0 copy-start.1
  1.6 1.1 %copy-done.1 = bf16[1,2,1536,128]{3,2,1,0:T(8,128)(2,1)S(1)} copy-done((bf16[1,2,1536,128]{3,2,1,0:T(8,128)(2,1)S(1)}, bf16[1,2,1536,128]{3,2,1,0:T(8,128)(2,1)}, u32[]{:S(2)}) %copy-start.1) | copy-done | bytes 786456
  2.7 0.0 copy-start.2
  2.7 1.1 %copy-done.2 = bf16[1,2,256,768]{3,2,1,0:T(8,128)(2,1)S(1)} copy-done((bf16[1,2,256,768]{3,2,1,0:T(8,128)(2,1)S(1)}, bf16[1,2,256,768]{3,2,1,0:T(8,128)(2,1)}, u32[]{:S(2)}) %copy-start.2) | copy-done | bytes 786456
  3.9 0.0 copy-start.3
  3.9 0.7 %copy-done.3 = s32[1,2,24]{2,1,0:T(2,128)S(1)} copy-done((s32[1,2,24]{2,1,0:T(2,128)S(1)}, s32[1,2,24]{2,1,0:T(2,128)}, u32[]{:S(2)}) %copy-start.3) | copy-done | bytes 216
  4.5 0.0 copy-start.4
  4.5 0.7 %copy-done.4 = s32[1,2]{1,0:T(1,128)S(1)} copy-done((s32[1,2]{1,0:T(1,128)S(1)}, s32[1,2]{1,0:T(1,128)}, u32[]{:S(2)}) %copy-start.4) | copy-done | bytes 32
  5.2 57.0 %shard_map.64 = f32[1,384,768]{2,1,0:T(8,128)S(1)} custom-call(bf16[1,1536,768]{2,1,0:T(8,128)(2,1)} %front_in.1, bf16[1,2,1536,128]{3,2,1,0:T(8,128)(2,1)S(1)} %copy-done.1, bf16[1,2,256,768]{3,2,1,0:T(8,128)(2,1)S(1)} %copy-done.2, f32[1,2,512,512]{3,2,1,0:T(8,128)S(1)} %copy-done, s32[1,2,24]{2,1,0:T(2,128)S(1)} %copy-done.3, s32[1,2]{1,0:T(1,128)S(1)} %copy-done.4), custom_call_target="tpu_custom_call" | custom-call | tf_op jit(solution)/shard_map/pallas_call | solution.py:348
  62.2 1.0 %copy.8 = f32[1,384,768]{2,1,0:T(8,128)} copy(f32[1,384,768]{2,1,0:T(8,128)S(1)} %shard_map.64) | data formatting | bytes 2359296
Async XLA Ops:
  0.0 1.6 %copy-start = (f32[1,2,512,512]{3,2,1,0:T(8,128)S(1)}, f32[1,2,512,512]{3,2,1,0:T(8,128)}, u32[]{:S(2)}) copy-start(f32[1,2,512,512]{3,2,1,0:T(8,128)} %diag_in.1) | copy-start | bytes 6291460
  1.6 1.1 %copy-start.1 = (bf16[1,2,1536,128]{3,2,1,0:T(8,128)(2,1)S(1)}, bf16[1,2,1536,128]{3,2,1,0:T(8,128)(2,1)}, u32[]{:S(2)}) copy-start(bf16[1,2,1536,128]{3,2,1,0:T(8,128)(2,1)} %lower_in.1) | copy-start | bytes 2359300
  2.7 1.1 %copy-start.2 = (bf16[1,2,256,768]{3,2,1,0:T(8,128)(2,1)S(1)}, bf16[1,2,256,768]{3,2,1,0:T(8,128)(2,1)}, u32[]{:S(2)}) copy-start(bf16[1,2,256,768]{3,2,1,0:T(8,128)(2,1)} %upper_in.1) | copy-start | bytes 2359300
  3.9 0.7 %copy-start.3 = (s32[1,2,24]{2,1,0:T(2,128)S(1)}, s32[1,2,24]{2,1,0:T(2,128)}, u32[]{:S(2)}) copy-start(s32[1,2,24]{2,1,0:T(2,128)} %fill.1) | copy-start | bytes 580
  4.5 0.7 %copy-start.4 = (s32[1,2]{1,0:T(1,128)S(1)}, s32[1,2]{1,0:T(1,128)}, u32[]{:S(2)}) copy-start(s32[1,2]{1,0:T(1,128)} %widths.1) | copy-start | bytes 28

commit v3 on v2

--- a/solution.py
+++ b/solution.py
@@ -10,22 +10,17 @@
 BLOCK = 128
 MESH = pl.DeviceIdType.MESH
 CHUNK = 256
-HEAD = 16
-
-
-def pack(values, ref):
-    rows, cols = values.shape
+
+
+def pack(values, ref, scale):
     top = jnp.maximum(jnp.max(jnp.abs(values), axis=0, keepdims=True), 1e-30)
     power = jnp.ceil(jnp.log2(top))
-    coded = jnp.round(values * jnp.exp2(14.0 - power))
-    ref[:HEAD, :] = jnp.broadcast_to(power, (HEAD, cols)).astype(jnp.int32).astype(jnp.int16)
-    ref[HEAD:, :] = coded.astype(jnp.int32).astype(jnp.int16)
-
-
-def unpack(ref):
-    power = ref[:HEAD, :].astype(jnp.int32).astype(jnp.float32)[:1, :]
-    coded = ref[HEAD:, :].astype(jnp.int32).astype(jnp.float32)
-    return coded * jnp.exp2(power - 14.0)
+    ref[...] = jnp.round(values * jnp.exp2(14.0 - power)).astype(jnp.int32).astype(jnp.int16)
+    scale[...] = jnp.exp2(power - 14.0)
+
+
+def unpack(ref, scale):
+    return ref[...].astype(jnp.int32).astype(jnp.float32) * scale[...]
 
 
 def split(values):
@@ -61,9 +56,9 @@
 def front_kernel(
     n, n_col, n_row, strip, chunks,
     front_in, lower_in, upper_in, diag_in, fill, widths, out,
-    front, lower_own, lower, upper, scaled, diag, inv, send, recv,
+    front, lower_own, lower, upper, scaled, diag, inv, send, recv, send_scale, recv_scale,
     load_sem, lower_send, lower_recv, upper_send, upper_recv, upper_load,
-    inv_send, inv_recv, send_sem, recv_sem,
+    inv_send, inv_recv, send_sem, recv_sem, scale_send, scale_recv,
 ):
     layer = lax.axis_index("layer")
     col = lax.axis_index("col")
@@ -72,7 +67,7 @@
     has_left = place > 0
     has_right = place < n - 1
     members, row_count, width = lower_own.shape
-    part = upper_in.shape[2]
+    part_rows = upper_in.shape[2]
     half = lax.rem(col, 2)
     mate = col + 1 - 2 * half
 
@@ -83,7 +78,7 @@
     diag_load.start()
 
     def upper_view(ref_row, j):
-        rows = pl.ds(pl.multiple_of(ref_row * part, part), part)
+        rows = pl.ds(pl.multiple_of(ref_row * part_rows, part_rows), part_rows)
         return upper.at[:, rows, pl.ds(pl.multiple_of(j * CHUNK, CHUNK), CHUNK)]
 
     def upper_copy(d, j):
@@ -106,7 +101,7 @@
             device_id_type=MESH,
         )
 
-    rows_own = pl.ds(pl.multiple_of(row * part, part), part)
+    rows_own = pl.ds(pl.multiple_of(row * part_rows, part_rows), part_rows)
     upper_own = pltpu.make_async_copy(upper_in.at[0], upper.at[:, rows_own, :], upper_load)
     upper_own.start()
     front_load.start()
@@ -230,15 +225,22 @@
             total = total - dot(lower[s, rows, :], scaled[s, :, cols])
         return total
 
-    def copy(way, k, j, target):
-        return pltpu.make_async_remote_copy(
-            src_ref=send.at[way, k, j],
-            dst_ref=recv.at[way, k, j],
-            send_sem=send_sem.at[way, k, j],
-            recv_sem=recv_sem.at[way, k, j],
-            device_id={"layer": target},
-            device_id_type=MESH,
-        )
+    def copies(way, k, j, target):
+        parts = (
+            (send_scale, recv_scale, scale_send, scale_recv),
+            (send, recv, send_sem, recv_sem),
+        )
+        return [
+            pltpu.make_async_remote_copy(
+                src_ref=source.at[way, k, j],
+                dst_ref=landing.at[way, k, j],
+                send_sem=out_sem.at[way, k, j],
+                recv_sem=in_sem.at[way, k, j],
+                device_id={"layer": target},
+                device_id_type=MESH,
+            )
+            for source, landing, out_sem, in_sem in parts
+        ]
 
     first = jnp.where(place * 2 < n, 0, 1)
 
@@ -269,14 +271,20 @@
 
             @pl.when(fed)
             def _():
-                copy(way, k, j, source).wait_recv()
-                pack(value + unpack(recv.at[way, k, j]), slot)
+                for part in copies(way, k, j, source):
+                    part.wait_recv()
+                pack(
+                    value + unpack(recv.at[way, k, j], recv_scale.at[way, k, j]),
+                    slot,
+                    send_scale.at[way, k, j],
+                )
 
             @pl.when(jnp.logical_not(fed))
             def _():
-                pack(value, slot)
-
-            copy(way, k, j, target).start()
+                pack(value, slot, send_scale.at[way, k, j])
+
+            for part in copies(way, k, j, target):
+                part.start()
 
         return 0
 
@@ -302,8 +310,11 @@
 
             @pl.when(fed)
             def _():
-                copy(way, k, j, source).wait_recv()
-                out[0, :, cols] = out[0, :, cols] + unpack(recv.at[way, k, j])
+                for part in copies(way, k, j, source):
+                    part.wait_recv()
+                out[0, :, cols] = out[0, :, cols] + unpack(
+                    recv.at[way, k, j], recv_scale.at[way, k, j]
+                )
 
         return 0
 
@@ -317,7 +328,8 @@
 
         @pl.when(k < count)
         def _():
-            copy(way, k, j, target).wait_send()
+            for part in copies(way, k, j, target):
+                part.wait_send()
 
         return 0
 
@@ -358,8 +370,10 @@
             pltpu.VMEM((members, order, cols), jnp.bfloat16),
             pltpu.VMEM((order, order), jnp.float32),
             pltpu.VMEM((members, 2, order, order), jnp.bfloat16),
-            pltpu.VMEM((2, n - 1, chunks, strip + HEAD, CHUNK), jnp.int16),
-            pltpu.VMEM((2, n - 1, chunks, strip + HEAD, CHUNK), jnp.int16),
+            pltpu.VMEM((2, n - 1, chunks, strip, CHUNK), jnp.int16),
+            pltpu.VMEM((2, n - 1, chunks, strip, CHUNK), jnp.int16),
+            pltpu.VMEM((2, n - 1, chunks, 1, CHUNK), jnp.float32),
+            pltpu.VMEM((2, n - 1, chunks, 1, CHUNK), jnp.float32),
             dma((3,)),
             dma((n_col - 1, n)),
             dma((n_col - 1, n)),
@@ -370,9 +384,11 @@
             dma,
             dma((2, n - 1, chunks)),
             dma((2, n - 1, chunks)),
+            dma((2, n - 1, chunks)),
+            dma((2, n - 1, chunks)),
         ],
         compiler_params=pltpu.CompilerParams(
-            collective_id=0, has_side_effects=True, vmem_limit_bytes=48 * 2**20
+            collective_id=0, has_side_effects=True, vmem_limit_bytes=60 * 2**20
         ),
     )(front, lower, upper, diag, fill, widths)
 

time: 63.5 us -> 59.9 us (0.943)
  local copies, waits for them, and re-layouts: 6.2 us -> 2.36 us
    unnamed x11 -> x1, local copies, waits for them, and re-layouts: 6.2 us -> 2.36 us
where the time goes in v3:
time: 59.9 us; the launch traced here: 59.7 us
  Pallas kernels  57.3 us (96%)
  local copies, waits for them, and re-layouts  2.36 us (4%)
    pallas_call x1, Pallas kernels, on_device(): pl.pallas_call(functools.partial(front_kernel, n, n_col, n_row, strip, ch...  57.3 us
    unnamed x1, local copies, waits for them, and re-layouts  2.36 us

profile of v3, /device:TPU:8, one launch (start us, length us, event | category | flops | bytes accessed | tf_op | source)
XLA Modules:
  0.0 59.7 jit_solution(7513159629746307742)
XLA Ops:
  0.0 57.3 %shard_map.64 = f32[1,384,768]{2,1,0:T(8,128)} custom-call(bf16[1,1536,768]{2,1,0:T(8,128)(2,1)} %front_in.1, bf16[1,2,1536,128]{3,2,1,0:T(8,128)(2,1)} %lower_in.1, bf16[1,2,256,768]{3,2,1,0:T(8,128)(2,1)} %upper_in.1, f32[1,2,512,512]{3,2,1,0:T(8,128)} %diag_in.1, s32[1,2,24]{2,1,0:T(2,128)} %fill.1, s32[1,2]{1,0:T(1,128)} %widths.1), custom_call_target="tpu_custom_call" | custom-call | tf_op jit(solution)/shard_map/pallas_call | solution.py:360
  57.3 2.4 %copy.8 = f32[1,384,768]{2,1,0:T(8,128)} copy(f32[1,384,768]{2,1,0:T(8,128)} %shard_map.64) | data formatting | bytes 2359296
